TPU v7x, 32 devices: a whole 2x2x4 slice. The times are simulated.
32 devices in a mesh: row: 8 (over z, x), col: 4 (over y, core).
Axes of the slice: x: 2, y: 2, z: 4, core: 2. Of those that a mesh axis runs over, the one named last changes fastest.
Arguments:
- sp2_branch: int32 [3], replicated, may hold values from 0 to 1, as said below
- p0_occupancy: int32 [8, 8], replicated, may hold values from 0 to 1, as said below
- p1_occupancy: int32 [8, 8], replicated, may hold values from 0 to 1, as said below
- p0_columns: bfloat16 [6144, 512], P('col'), as said below
- p1_tiles: bfloat16 [3, 2048, 2048], P(None, 'row', 'col'), may hold values from -6 to 6, as said below
Outputs:
- p1_next: bfloat16 [3, 2048, 2048], P(None, 'row', 'col')
Inputs may be any that keep to these rules, and one draw needn't show every extreme that they name: `sp2_branch`: both values occur among the displacements. `p0_occupancy`: symmetric; every diagonal block is 1; blocks more than 2 apart around the circle of 8 blocks are 0. `p1_occupancy`: symmetric. `p0_columns`: the strips describe one symmetric matrix: a stored entry at row u and column v equals the stored entry at row v and column u; blocks more than 2 apart around the circle are zero. `p1_tiles`: each displacement's matrix is symmetric.
All inputs are finite; a program needn't handle non-finite values.
Results may differ from a plain program's by a relative error of at most 0.001.
Values may be sent and summed in bfloat16 or wider, within the bound.
A program may use at most 192 MiB of HBM per device.

v0:
```python
import jax
import jax.numpy as jnp
from jax import lax
from jax.sharding import PartitionSpec as P

BLK = 256


def from_behind(array, axis, by):
    length = lax.axis_size(axis)
    return lax.ppermute(array, axis, [(i, (i + by) % length) for i in range(length)])


def broadcast(array, axis, root):
    mine = lax.axis_index(axis) == root
    return lax.psum(jnp.where(mine, array, jnp.zeros_like(array)), axis)


def mask_blocks(values, occupancy):
    leading = values.shape[:-2]
    row_blocks = values.shape[-2] // BLK
    col_blocks = values.shape[-1] // BLK
    shaped = values.reshape(leading + (row_blocks, BLK, col_blocks, BLK))
    weight = occupancy.astype(values.dtype)[:, None, :, None]
    return (shaped * weight).reshape(values.shape)


def right_product(left_op, right_op):
    return jnp.einsum("drc,ck->drk", left_op, right_op, preferred_element_type=jnp.float32)


def left_product(left_op, right_op):
    return jnp.einsum("kr,dkc->drc", left_op, right_op, preferred_element_type=jnp.float32)


def column_term(summed, incoming, factor):
    return summed + right_product(incoming, factor)


def row_term(summed, incoming, factor):
    return summed + left_product(factor, incoming)


def col_move(values, distance):
    return from_behind(values, "col", distance)


def row_move(values, distance):
    return from_behind(values, "row", distance)


def body(sp2_branch, p0_occupancy, p1_occupancy, p0_columns, p1_tiles):
    col_count = lax.axis_size("col")
    col_width = p0_columns.shape[1]
    row_height = p1_tiles.shape[1]
    col_blocks = col_width // BLK
    row_blocks = row_height // BLK
    strip_blocks = p0_columns.shape[0] // BLK
    band_half = (strip_blocks - col_blocks) // 2
    all_blocks = col_blocks * col_count
    col_span = band_half // col_blocks
    row_span = band_half // row_blocks
    row_at = lax.axis_index("row")
    col_at = lax.axis_index("col")
    own_occ = lax.dynamic_slice(
        p1_occupancy, (row_at * row_blocks, col_at * col_blocks), (row_blocks, col_blocks)
    )
    p1_local = mask_blocks(p1_tiles, own_occ)
    tripled = jnp.concatenate([p0_occupancy, p0_occupancy, p0_occupancy], axis=0)
    strip_occ = lax.dynamic_slice(
        tripled,
        (col_at * col_blocks - band_half + all_blocks, col_at * col_blocks),
        (strip_blocks, col_blocks),
    )
    strip_local = mask_blocks(p0_columns, strip_occ)

    def col_add(summed, incoming, distance):
        factor = strip_local[
            (distance + col_span) * col_width : (distance + col_span + 1) * col_width, :
        ]
        return column_term(summed, incoming, factor)

    summed_col = jnp.zeros(p1_local.shape, jnp.float32)
    summed_col = col_add(summed_col, p1_local, 0)
    moving = p1_local
    for distance in range(1, col_span + 1):
        moving = col_move(moving, 1)
        summed_col = col_add(summed_col, moving, -distance)
    moving = from_behind(moving, "col", -2 * col_span)
    summed_col = col_add(summed_col, moving, col_span)
    for distance in range(col_span - 1, 0, -1):
        moving = col_move(moving, 1)
        summed_col = col_add(summed_col, moving, distance)
    owner_col = row_at * row_blocks // col_blocks
    offset_blocks = row_at * row_blocks - owner_col * col_blocks
    shared = broadcast(strip_local, "col", owner_col)
    row_part = lax.dynamic_slice(
        shared,
        (offset_blocks * BLK, offset_blocks * BLK),
        ((row_blocks + 2 * band_half) * BLK, row_height),
    )

    def row_add(summed, incoming, distance):
        factor = row_part[
            (distance + row_span) * row_height : (distance + row_span + 1) * row_height, :
        ]
        return row_term(summed, incoming, factor)

    summed_row = jnp.zeros(p1_local.shape, jnp.float32)
    summed_row = row_add(summed_row, p1_local, 0)
    moving = p1_local
    for distance in range(1, row_span + 1):
        moving = row_move(moving, 1)
        summed_row = row_add(summed_row, moving, -distance)
    moving = from_behind(moving, "row", -2 * row_span)
    summed_row = row_add(summed_row, moving, row_span)
    for distance in range(row_span - 1, 0, -1):
        moving = row_move(moving, 1)
        summed_row = row_add(summed_row, moving, distance)
    bracket = summed_col + summed_row
    squared = (sp2_branch == 1)[:, None, None]
    chosen = jnp.where(squared, bracket, 2.0 * p1_local.astype(jnp.float32) - bracket)
    return mask_blocks(chosen, own_occ).astype(jnp.bfloat16)


def solution(mesh):
    in_specs = (P(), P(), P(), P("col", None), P(None, "row", "col"))
    out_specs = P(None, "row", "col")
    return jax.shard_map(body, mesh=mesh, in_specs=in_specs, out_specs=out_specs, check_vma=False)
```

profile of v0, /device:TPU:0, one launch (start us, length us, event | category | flops | bytes accessed | tf_op | source)
XLA Modules:
  0.0 119.0 jit_solution(12763739331983620217)
XLA Ops:
  6.5 0.8 convert_bitcast_fusion
  7.3 0.1 broadcast_bitcast_fusion.1
  7.4 1.2 broadcast_multiply_fusion.1
  8.6 3.0 %collective-permute-start.2 = (bf16[3,256,512]{2,1,0:T(8,128)(2,1)S(1)}, bf16[3,256,512]{2,1,0:T(8,128)(2,1)}, u32[]{:S(2)}, u32[]{:S(2)}) collective-permute-start(bf16[3,256,512]{2,1,0:T(8,128)(2,1)S(1)} %broadcast_multiply_fusion.1), channel_id=1, source_target_pairs={{0,4},{4,8},{8,12},{12,16},{16,20},{20,24},{24,28},{28,0},{1,5},{5... | collective-permute-start | bytes 2359304 | tf_op jit(solution)/shard_map/ppermute | solution.py:11
  11.7 0.1 pad_add_fusion
  11.7 0.1 dynamic-slice_convert_fusion
  11.8 0.1 copy.19
  11.9 0.9 mul.71
  12.8 0.4 copy.41
  13.2 1.0 copy-done
  14.2 1.4 %multiply_select_fusion = bf16[1536,512]{1,0:T(8,128)(2,1)} fusion(bf16[1536,512]{1,0:T(8,128)(2,1)S(1)} %copy-done, bf16[1536,512]{1,0:T(8,128)(2,1)S(1)} %bitcast.43, pred[]{:T(512)S(6)} %eq.7), kind=kLoop, calls=%fused_computation.4 | loop fusion | flops 1572864 | bytes 4718593 | tf_op jit(solution)/shard_map/jit(_where)/select_n | solution.py:16
  15.6 1.9 %reshape.28 = bf16[6,256,2,256]{3,2,1,0:T(2,128)(2,1)} reshape(bf16[1536,512]{1,0:T(8,128)(2,1)S(1)} %copy-done) | data formatting | bytes 3145728 | tf_op jit(solution)/shard_map/reshape | solution.py:23
  17.6 2.8 %broadcast_multiply_fusion = bf16[6,256,2,256]{3,2,1,0:T(2,128)(2,1)S(1)} fusion(bf16[6,256,2,256]{3,2,1,0:T(2,128)(2,1)} %reshape.28, bf16[6,2]{1,0:T(8,128)(2,1)S(1)} %copy.19), kind=kLoop, calls=%fused_computation.5 | loop fusion | flops 786432 | bytes 3145752 | tf_op jit(solution)/shard_map/mul | solution.py:25
  20.4 11.9 %collective-permute-done.2 = bf16[3,256,512]{2,1,0:T(8,128)(2,1)} collective-permute-done((bf16[3,256,512]{2,1,0:T(8,128)(2,1)S(1)}, bf16[3,256,512]{2,1,0:T(8,128)(2,1)}, u32[]{:S(2)}, u32[]{:S(2)}) %collective-permute-start.2) | collective-permute-done | bytes 786464 | tf_op jit(solution)/shard_map/ppermute | solution.py:11
  32.3 1.1 fusion.6
  33.4 0.3 reshape.30
  33.7 0.3 reshape.31
  34.0 1.1 reshape.29
  35.2 1.6 %fusion.7 = f32[3,256,512]{2,1,0:T(8,128)S(1)} fusion(bf16[3,256,512]{2,1,0:T(8,128)(2,1)S(1)} %broadcast_multiply_fusion.1, bf16[512,512,1]{1,0,2:T(8,128)(2,1)} %reshape.29), kind=kOutput, calls=%fused_computation.24 | convolution fusion | flops 402653184 | bytes 2883584 | tf_op jit(solution)/shard_map/drc,ck->drk/dot_general | solution.py:29
  36.8 1.6 %collective-permute-start.1 = (bf16[3,256,512]{2,1,0:T(8,128)(2,1)}, bf16[3,256,512]{2,1,0:T(8,128)(2,1)}, u32[]{:S(2)}, u32[]{:S(2)}) collective-permute-start(bf16[3,256,512]{2,1,0:T(8,128)(2,1)} %collective-permute-done), channel_id=1, source_target_pairs={{0,2},{1,3},{2,0},{3,1},{4,6},{5,7},{6,4},{7,5},{8,10},{9,11},{10,... | collective-permute-start | bytes 2359304 | tf_op jit(solution)/shard_map/ppermute | solution.py:11
  38.4 16.6 %collective-permute-done.3 = bf16[3,256,512]{2,1,0:T(8,128)(2,1)} collective-permute-done((bf16[3,256,512]{2,1,0:T(8,128)(2,1)}, bf16[3,256,512]{2,1,0:T(8,128)(2,1)}, u32[]{:S(2)}, u32[]{:S(2)}) %collective-permute-start.3) | collective-permute-done | bytes 786464 | tf_op jit(solution)/shard_map/ppermute | solution.py:11
  55.0 13.8 %all-reduce.2.cloned.1.call-done = bf16[1536,512]{1,0:T(8,128)(2,1)} async-done(((bf16[1536,512]{1,0:T(8,128)(2,1)}), bf16[1536,512]{1,0:T(8,128)(2,1)}) %all-reduce.2.cloned.1.call-update) | async-done | bytes 1572880 | tf_op jit(solution)/shard_map/psum | solution.py:16
  68.8 1.5 %fusion.4 = f32[3,512,256]{1,2,0:T(8,128)S(1)} fusion(bf16[3,256,512]{2,1,0:T(8,128)(2,1)} %collective-permute-done.2, bf16[1536,512]{1,0:T(8,128)(2,1)} %all-reduce.2.cloned.1.call-done, s32[]{:T(128)S(6)} %add.73, s32[]{:T(128)S(6)} %select_n.40), kind=kOutput, calls=%fused_computation.13 | convolution fusion | flops 201326592 | bytes 2490376 | tf_op jit(solution)/shard_map/kr,dkc->drc/dot_general | solution.py:33
  70.4 1.3 %fusion.5 = f32[3,512,256]{1,2,0:T(8,128)S(1)} fusion(bf16[3,256,512]{2,1,0:T(8,128)(2,1)S(1)} %broadcast_multiply_fusion.1, bf16[1536,512]{1,0:T(8,128)(2,1)} %all-reduce.2.cloned.1.call-done, s32[]{:T(128)S(6)} %add.72, s32[]{:T(128)S(6)} %select_n.40), kind=kOutput, calls=%fused_computation.15 | convolution fusion | flops 201326592 | bytes 2490376 | tf_op jit(solution)/shard_map/kr,dkc->drc/dot_general | solution.py:33
  71.7 1.7 %fusion.8 = f32[3,256,512]{2,1,0:T(8,128)S(1)} fusion(bf16[3,256,512]{2,1,0:T(8,128)(2,1)} %collective-permute-done, bf16[512,512,1]{1,0,2:T(8,128)(2,1)S(1)} %reshape.30), kind=kOutput, calls=%fused_computation.25 | convolution fusion | flops 402653184 | bytes 2883584 | tf_op jit(solution)/shard_map/drc,ck->drk/dot_general | solution.py:29
  73.4 13.2 %collective-permute-done.4 = bf16[3,256,512]{2,1,0:T(8,128)(2,1)} collective-permute-done((bf16[3,256,512]{2,1,0:T(8,128)(2,1)}, bf16[3,256,512]{2,1,0:T(8,128)(2,1)}, u32[]{:S(2)}, u32[]{:S(2)}) %collective-permute-start.4) | collective-permute-done | bytes 786464 | tf_op jit(solution)/shard_map/ppermute | solution.py:11
  86.6 1.7 %collective-permute-start.5 = (bf16[3,256,512]{2,1,0:T(8,128)(2,1)}, bf16[3,256,512]{2,1,0:T(8,128)(2,1)S(1)}, u32[]{:S(2)}, u32[]{:S(2)}) collective-permute-start(bf16[3,256,512]{2,1,0:T(8,128)(2,1)} %collective-permute-done.4), channel_id=1, source_target_pairs={{0,4},{4,8},{8,12},{12,16},{16,20},{20,24},{24,28},{28,0},{1,5},{5... | collective-permute-start | bytes 2359304 | tf_op jit(solution)/shard_map/ppermute | solution.py:11
  88.3 1.5 %fusion.3 = f32[3,512,256]{1,2,0:T(8,128)S(1)} fusion(bf16[3,256,512]{2,1,0:T(8,128)(2,1)} %collective-permute-done.3, bf16[1536,512]{1,0:T(8,128)(2,1)} %all-reduce.2.cloned.1.call-done, s32[]{:T(128)S(6)} %select_n.39, s32[]{:T(128)S(6)} %select_n.40), kind=kOutput, calls=%fused_computation.11 | convolution fusion | flops 201326592 | bytes 2490376 | tf_op jit(solution)/shard_map/kr,dkc->drc/dot_general | solution.py:33
  89.8 1.7 %fusion.9 = f32[3,256,512]{2,1,0:T(8,128)S(1)} fusion(bf16[3,256,512]{2,1,0:T(8,128)(2,1)} %collective-permute-done.1, bf16[512,512,1]{1,0,2:T(8,128)(2,1)S(1)} %reshape.31), kind=kOutput, calls=%fused_computation.26 | convolution fusion | flops 402653184 | bytes 2883584 | tf_op jit(solution)/shard_map/drc,ck->drk/dot_general | solution.py:29
  91.5 1.6 %fusion.2 = f32[3,512,256]{1,2,0:T(8,128)S(1)} fusion(bf16[3,256,512]{2,1,0:T(8,128)(2,1)} %collective-permute-done.4, bf16[1536,512]{1,0:T(8,128)(2,1)} %all-reduce.2.cloned.1.call-done, s32[]{:T(128)S(6)} %add.74, s32[]{:T(128)S(6)} %select_n.40), kind=kOutput, calls=%fused_computation.9 | convolution fusion | flops 201326592 | bytes 2490376 | tf_op jit(solution)/shard_map/kr,dkc->drc/dot_general | solution.py:33
  93.1 15.8 %collective-permute-done.5 = bf16[3,256,512]{2,1,0:T(8,128)(2,1)S(1)} collective-permute-done((bf16[3,256,512]{2,1,0:T(8,128)(2,1)}, bf16[3,256,512]{2,1,0:T(8,128)(2,1)S(1)}, u32[]{:S(2)}, u32[]{:S(2)}) %collective-permute-start.5) | collective-permute-done | bytes 786464 | tf_op jit(solution)/shard_map/ppermute | solution.py:11
  108.9 3.2 %fusion.1 = bf16[3,256,512]{2,1,0:T(8,128)(2,1)} fusion(bf16[3,256,512]{2,1,0:T(8,128)(2,1)S(1)} %broadcast_multiply_fusion.1, f32[3,512,256]{1,2,0:T(8,128)S(1)} %fusion.2, f32[3,512,256]{1,2,0:T(8,128)S(1)} %fusion.3, f32[3,512,256]{1,2,0:T(8,128)S(1)} %fusion.5, f32[3,512,256]{1,2,0:T(8,128)S(1)} %fusion.4, f32[3,256,512]{2,1,0:T(8,128)S(1)} %fusion.9, ...), kind=kOutput, calls=%fused_computation.2 | convolution fusion | flops 206438400 | bytes 13502475 | tf_op jit(solution)/shard_map/kr,dkc->drc/dot_general | solution.py:33
  (17 shorter events, 0.2 us)
Async XLA Ops:
  6.5 5.0 %copy-start.1 = (s32[8,8]{1,0:T(8,128)S(1)}, s32[8,8]{1,0:T(8,128)}, u32[]{:S(2)}) copy-start(s32[8,8]{1,0:T(8,128)} %param.6) | copy-start | bytes 772
  6.5 62.3 %all-reduce.2.cloned.1.call-start = ((), (), s32[]{:S(2)}) async-start(), calls=%async_computation | async-start | bytes 3145728 | tf_op jit(solution)/shard_map/psum | solution.py:16
  8.6 23.7 %collective-permute-start.2 = (bf16[3,256,512]{2,1,0:T(8,128)(2,1)S(1)}, bf16[3,256,512]{2,1,0:T(8,128)(2,1)}, u32[]{:S(2)}, u32[]{:S(2)}) collective-permute-start(bf16[3,256,512]{2,1,0:T(8,128)(2,1)S(1)} %broadcast_multiply_fusion.1), channel_id=1, source_target_pairs={{0,4},{4,8},{8,12},{12,16},{16,20},{20,24},{24,28},{28,0},{1,5},{5... | collective-permute-start | bytes 2359304 | tf_op jit(solution)/shard_map/ppermute | solution.py:11
  11.6 25.2 %collective-permute-start = (bf16[3,256,512]{2,1,0:T(8,128)(2,1)S(1)}, bf16[3,256,512]{2,1,0:T(8,128)(2,1)}, u32[]{:S(2)}, u32[]{:S(2)}) collective-permute-start(bf16[3,256,512]{2,1,0:T(8,128)(2,1)S(1)} %broadcast_multiply_fusion.1), channel_id=1, source_target_pairs={{0,1},{1,2},{2,3},{3,0},{4,5},{5,6},{6,7},{7,4},{8,9},{9,10},{10,1... | collective-permute-start | bytes 2359304 | tf_op jit(solution)/shard_map/ppermute | solution.py:11
  12.8 1.4 %copy-start = (bf16[1536,512]{1,0:T(8,128)(2,1)S(1)}, bf16[1536,512]{1,0:T(8,128)(2,1)}, u32[]{:S(2)}) copy-start(bf16[1536,512]{1,0:T(8,128)(2,1)} %param.8) | copy-start | bytes 4718596
  32.3 22.7 %collective-permute-start.3 = (bf16[3,256,512]{2,1,0:T(8,128)(2,1)}, bf16[3,256,512]{2,1,0:T(8,128)(2,1)}, u32[]{:S(2)}, u32[]{:S(2)}) collective-permute-start(bf16[3,256,512]{2,1,0:T(8,128)(2,1)} %collective-permute-done.2), channel_id=1, source_target_pairs={{0,4},{4,8},{8,12},{12,16},{16,20},{20,24},{24,28},{28,0},{1,5},{5... | collective-permute-start | bytes 2359304 | tf_op jit(solution)/shard_map/ppermute | solution.py:11
  33.3 1.8 %copy-start.2 = (s32[3]{0:T(128)S(1)}, s32[3]{0:T(128)}, u32[]{:S(2)}) copy-start(s32[3]{0:T(128)} %param.5) | copy-start | bytes 40
  36.8 53.0 %collective-permute-start.1 = (bf16[3,256,512]{2,1,0:T(8,128)(2,1)}, bf16[3,256,512]{2,1,0:T(8,128)(2,1)}, u32[]{:S(2)}, u32[]{:S(2)}) collective-permute-start(bf16[3,256,512]{2,1,0:T(8,128)(2,1)} %collective-permute-done), channel_id=1, source_target_pairs={{0,2},{1,3},{2,0},{3,1},{4,6},{5,7},{6,4},{7,5},{8,10},{9,11},{10,... | collective-permute-start | bytes 2359304 | tf_op jit(solution)/shard_map/ppermute | solution.py:11
  55.0 31.6 %collective-permute-start.4 = (bf16[3,256,512]{2,1,0:T(8,128)(2,1)}, bf16[3,256,512]{2,1,0:T(8,128)(2,1)}, u32[]{:S(2)}, u32[]{:S(2)}) collective-permute-start(bf16[3,256,512]{2,1,0:T(8,128)(2,1)} %collective-permute-done.3), channel_id=1, source_target_pairs={{0,16},{4,20},{8,24},{12,28},{16,0},{20,4},{24,8},{28,12},{1,17},{... | collective-permute-start | bytes 2359304 | tf_op jit(solution)/shard_map/ppermute | solution.py:11
  86.6 22.4 %collective-permute-start.5 = (bf16[3,256,512]{2,1,0:T(8,128)(2,1)}, bf16[3,256,512]{2,1,0:T(8,128)(2,1)S(1)}, u32[]{:S(2)}, u32[]{:S(2)}) collective-permute-start(bf16[3,256,512]{2,1,0:T(8,128)(2,1)} %collective-permute-done.4), channel_id=1, source_target_pairs={{0,4},{4,8},{8,12},{12,16},{16,20},{20,24},{24,28},{28,0},{1,5},{5... | collective-permute-start | bytes 2359304 | tf_op jit(solution)/shard_map/ppermute | solution.py:11
Sparse Core Ops, SparseCore 0:
  15.7 53.0 all-reduce.1
where the time goes:
time: 119 us
  waiting for transfers between devices  71.3 us (60%)
  matrix products  14.2 us (12%)
  between operations  13.5 us (11%)
  local copies, waits for them, and re-layouts  7.38 us (6%)
  starting transfers between devices  6.29 us (5%)
  other arithmetic  6.28 us (5%)
    ppermute x6, waiting for transfers between devices, from_behind(): lax.ppermute(array, axis, [(i, (i + by) % length) for i in range(length)])  57.5 us
    psum x1, waiting for transfers between devices, broadcast(): return lax.psum(jnp.where(mine, array, jnp.zeros_like(array)), axis)  13.8 us
    dot_general x5, matrix products, left_product(): jnp.einsum('kr,dkc->drc', left_op, right_op, preferred_element_type=jnp.f...  9.14 us
    ppermute x6, starting transfers between devices, from_behind(): lax.ppermute(array, axis, [(i, (i + by) % length) for i in range(length)])  6.29 us
    dot_general x3, matrix products, right_product(): jnp.einsum('drc,ck->drk', left_op, right_op, preferred_element_type=jnp.f...  5.02 us
    mul x3, other arithmetic, mask_blocks(): return (shaped * weight).reshape(values.shape)  4.76 us
    slice x4, local copies, waits for them, and re-layouts, col_add(): strip_local[(distance + col_span) * col_width:(distance + col_span + 1) *...  2.87 us
  transfers between devices with their start and end apart: 7, of which 5 were waited for; matrix products, arithmetic and copies ran while one was open for 18% of the time, Pallas kernels for 0%

commit v1 on v0

v1 whole, which is shorter than its diff:
```python
import functools

import jax
import jax.numpy as jnp
from jax import lax
from jax.experimental import pallas as pl
from jax.experimental.pallas import tpu as pltpu
from jax.sharding import PartitionSpec as P

BLK = 256
MESH = pl.DeviceIdType.MESH


def mask_into(dst, src, occ, row_block, col_block, total):
    rows, cols = src.shape[-2], src.shape[-1]
    for i in range(rows // BLK):
        for j in range(cols // BLK):
            weight = occ[lax.rem(row_block + i + total, total), col_block + j].astype(jnp.float32)
            at = (slice(i * BLK, (i + 1) * BLK), slice(j * BLK, (j + 1) * BLK))
            at = (slice(None),) * (len(src.shape) - 2) + at
            dst[at] = (src[at].astype(jnp.float32) * weight).astype(jnp.bfloat16)


def kernel(
    row_count, col_count, relay,
    branch, p0_occ, p1_occ, strip_in, tile_in, out,
    mine, strip, fact, acc, cols, rows,
    col_send, col_recv, row_send, row_recv, fact_send, fact_recv,
):
    disp, height, width = tile_in.shape
    row_blocks, col_blocks = height // BLK, width // BLK
    total = col_count * col_blocks
    half = (strip_in.shape[0] // BLK - col_blocks) // 2
    col_span, row_span = half // col_blocks, half // row_blocks
    r, c = lax.axis_index("row"), lax.axis_index("col")
    odd = lax.rem(r, 2)

    def row_id(distance):
        return (lax.rem(r + distance + row_count, row_count), c)

    def col_id(distance):
        return (r, lax.rem(c + distance + col_count, col_count))

    row_far = [t for t in range(-row_span, row_span + 1) if t]
    col_far = [t for t in range(-col_span, col_span + 1) if t]
    partner = row_id(1 - 2 * odd)
    greeted = [col_id(t) for t in range(1, col_count)]
    greeted += [row_id(2), row_id(-2), partner] if relay else [row_id(t) for t in row_far]
    barrier = pltpu.get_barrier_semaphore()
    for device in greeted:
        pl.semaphore_signal(barrier, inc=1, device_id=device, device_id_type=MESH)

    mask_into(mine, tile_in, p1_occ, r * row_blocks, c * col_blocks, total)
    pl.semaphore_wait(barrier, len(greeted))

    def remote(src, dst, send, recv, device):
        return pltpu.make_async_remote_copy(
            src_ref=src, dst_ref=dst, send_sem=send, recv_sem=recv,
            device_id=device, device_id_type=MESH,
        )

    def z_copy(which, d):
        return remote(mine.at[d], rows.at[3 * which, d], row_send.at[which, d],
                      row_recv.at[which, d], row_id(2 - 4 * which))

    def own_copy(d):
        return remote(mine.at[d], rows.at[1 + odd, d], row_send.at[2, d],
                      row_recv.at[2, d], partner)

    def relay_copy(d):
        return remote(rows.at[3 - 3 * odd, d], rows.at[2 - odd, d], row_send.at[3, d],
                      row_recv.at[3, d], partner)

    def row_copy(k, d):
        return remote(mine.at[d], rows.at[len(row_far) - 1 - k, d],
                      row_send.at[len(row_far) - 1 - k, d],
                      row_recv.at[len(row_far) - 1 - k, d], row_id(row_far[k]))

    def col_copy(k):
        back = len(col_far) - 1 - k
        return remote(mine, cols.at[back], col_send.at[back], col_recv.at[back],
                      col_id(col_far[k]))

    if relay:
        for d in range(disp):
            z_copy(0, d).start()
            z_copy(1, d).start()
        for d in range(disp):
            own_copy(d).start()
    else:
        for d in range(disp):
            for k in range(len(row_far)):
                row_copy(k, d).start()

    mask_into(strip, strip_in, p0_occ, c * col_blocks - half, c * col_blocks, total)
    owner = r * row_blocks // col_blocks
    offset = pl.multiple_of((r * row_blocks - owner * col_blocks) * BLK, BLK)

    def fact_copy(k):
        return remote(fact, fact, fact_send.at[k], fact_recv.at[0], col_id(k + 1))

    @pl.when(c == owner)
    def _():
        for k in range(fact.shape[1] // BLK):
            for i in range(row_blocks):
                block = strip[pl.ds(offset + k * BLK, BLK), pl.ds(offset + i * BLK, BLK)]
                fact[i * BLK:(i + 1) * BLK, k * BLK:(k + 1) * BLK] = block.T
        for k in range(col_count - 1):
            fact_copy(k).start()

    for k in range(len(col_far)):
        col_copy(k).start()

    def col_add(tile, distance, first=False):
        at = pl.ds(pl.multiple_of((distance + col_span) * width, BLK), width)

        def step(d, carry):
            term = jnp.dot(tile[d], strip[at, :], preferred_element_type=jnp.float32)
            acc[d] = term if first else acc[d] + term
            return carry

        lax.fori_loop(0, disp, step, 0)

    def row_term(tile, distance, d):
        at = pl.ds(pl.multiple_of((distance + row_span) * height, BLK), height)
        return jnp.dot(fact[:, at], tile[d], preferred_element_type=jnp.float32)

    def row_add(tile, distance):
        def step(d, carry):
            acc[d] += row_term(tile, distance, d)
            return carry

        lax.fori_loop(0, disp, step, 0)

    def finish(d):
        squared = branch[d].astype(jnp.float32)
        for i in range(row_blocks):
            for j in range(col_blocks):
                at = (d, slice(i * BLK, (i + 1) * BLK), slice(j * BLK, (j + 1) * BLK))
                weight = p1_occ[r * row_blocks + i, c * col_blocks + j].astype(jnp.float32)
                own = mine[at].astype(jnp.float32) * (2.0 - 2.0 * squared)
                value = own + acc[at] * (2.0 * squared - 1.0)
                out[at] = (value * weight).astype(jnp.bfloat16)

    def wait_fact():
        @pl.when(c != owner)
        def _():
            fact_copy(0).wait_recv()

    col_add(mine, 0, first=True)
    if relay:
        def forward(d):
            remote(mine.at[d], rows.at[0, d], row_send.at[0, d],
                   row_recv.at[1 - odd, d], partner).wait_recv()
            relay_copy(d).start()

        forward(0)
        wait_fact()
        row_add(mine, 0)
        forward(1)
        for k in range(len(col_far)):
            col_copy(len(col_far) - 1 - k).wait_recv()
            col_add(cols.at[k], col_far[k])
        for d in range(disp):
            own_copy(d).wait_recv()
        row_add(rows.at[2 - odd], 1 - 2 * odd)
        for d in range(2, disp):
            forward(d)
        row_add(rows.at[3 - 3 * odd], 2 - 4 * odd)
        for d in range(disp):
            remote(mine.at[d], rows.at[0, d], row_send.at[0, d],
                   row_recv.at[odd, d], partner).wait_recv()
        row_add(rows.at[3 * odd], 4 * odd - 2)
        for d in range(disp):
            relay_copy(d).wait_recv()
            acc[d] += row_term(rows.at[1 + odd], 2 * odd - 1, d)
            finish(d)
    else:
        wait_fact()
        row_add(mine, 0)
        for k in range(len(col_far)):
            col_copy(k).wait_recv()
            col_add(cols.at[len(col_far) - 1 - k], col_far[len(col_far) - 1 - k])
        for k in range(len(row_far)):
            for d in range(disp):
                row_copy(k, d).wait_recv()
            row_add(rows.at[len(row_far) - 1 - k], row_far[len(row_far) - 1 - k])
        for d in range(disp):
            finish(d)

    for k in range(len(col_far)):
        col_copy(k).wait_send()
    for d in range(disp):
        if relay:
            z_copy(0, d).wait_send()
            z_copy(1, d).wait_send()
            own_copy(d).wait_send()
            relay_copy(d).wait_send()
        else:
            for k in range(len(row_far)):
                row_copy(k, d).wait_send()

    @pl.when(c == owner)
    def _():
        for k in range(col_count - 1):
            fact_copy(k).wait_send()


def body(sp2_branch, p0_occupancy, p1_occupancy, p0_columns, p1_tiles):
    row_count, col_count = lax.axis_size("row"), lax.axis_size("col")
    disp, height, width = p1_tiles.shape
    strip_rows = p0_columns.shape[0]
    half = (strip_rows - width) // 2
    row_slots, col_slots = 2 * (half // height), 2 * (half // width)
    bf16 = jnp.bfloat16
    relay = row_slots == 4
    flops = 2 * disp * height * width * (strip_rows + height + 2 * half)
    return pl.pallas_call(
        functools.partial(kernel, row_count, col_count, relay),
        out_shape=jax.ShapeDtypeStruct(p1_tiles.shape, bf16),
        in_specs=[pl.BlockSpec(memory_space=pltpu.SMEM)] * 3
        + [pl.BlockSpec(memory_space=pltpu.VMEM)] * 2,
        out_specs=pl.BlockSpec(memory_space=pltpu.VMEM),
        scratch_shapes=[
            pltpu.VMEM((disp, height, width), bf16),
            pltpu.VMEM(p0_columns.shape, bf16),
            pltpu.VMEM((height, height + 2 * half), bf16),
            pltpu.VMEM((disp, height, width), jnp.float32),
            pltpu.VMEM((col_slots, disp, height, width), bf16),
            pltpu.VMEM((row_slots, disp, height, width), bf16),
            pltpu.SemaphoreType.DMA((col_slots,)),
            pltpu.SemaphoreType.DMA((col_slots,)),
            pltpu.SemaphoreType.DMA((row_slots, disp)),
            pltpu.SemaphoreType.DMA((row_slots, disp)),
            pltpu.SemaphoreType.DMA((col_count - 1,)),
            pltpu.SemaphoreType.DMA((1,)),
        ],
        compiler_params=pltpu.CompilerParams(
            collective_id=0, has_side_effects=True, vmem_limit_bytes=58 * 1024 * 1024
        ),
        cost_estimate=pl.CostEstimate(flops=flops, bytes_accessed=4 << 20, transcendentals=0),
    )(sp2_branch, p0_occupancy, p1_occupancy, p0_columns, p1_tiles)


def solution(mesh):
    in_specs = (P(), P(), P(), P("col", None), P(None, "row", "col"))
    out_specs = P(None, "row", "col")
    return jax.shard_map(body, mesh=mesh, in_specs=in_specs, out_specs=out_specs, check_vma=False)
```

time: 119 us -> 49.9 us (0.42)
  waiting for transfers between devices: 71.3 us -> 0 us
  Pallas kernels: 0 us -> 47.6 us
  matrix products: 14.2 us -> 0 us
  between operations: 13.5 us -> 0.01 us
  starting transfers between devices: 6.29 us -> 0 us
  other arithmetic: 6.28 us -> 0 us
  local copies, waits for them, and re-layouts: 7.38 us -> 2.06 us
    ppermute x6 -> x0, waiting for transfers between devices: 57.5 us -> none  [from_behind(): lax.ppermute(array, axis, [(i, (i + by) % length) for i in range(length)])]
    pallas_call x0 -> x1, Pallas kernels: none -> 47.6 us  [body(): pl.pallas_call(functools.partial(kernel, row_count, col_count, relay), ou...]
    dot_general x8 -> x0, matrix products: 14.2 us -> none  [the longest x5 9.14 us: left_product(): jnp.einsum('kr,dkc->drc', left_op, right_op, preferred_element_type=jnp.f...]
    psum x1 -> x0, waiting for transfers between devices: 13.8 us -> none  [broadcast(): return lax.psum(jnp.where(mine, array, jnp.zeros_like(array)), axis)]
    ppermute x6 -> x0, starting transfers between devices: 6.29 us -> none  [from_behind(): lax.ppermute(array, axis, [(i, (i + by) % length) for i in range(length)])]
    mul x3 -> x0, other arithmetic: 4.76 us -> none  [mask_blocks(): return (shaped * weight).reshape(values.shape)]
    slice x4 -> x0, local copies, waits for them, and re-layouts: 2.87 us -> none  [col_add(): strip_local[(distance + col_span) * col_width:(distance + col_span + 1) *...]
    reshape x1 -> x0, local copies, waits for them, and re-layouts: 1.89 us -> none  [mask_blocks(): shaped = values.reshape(leading + (row_blocks, BLK, col_blocks, BLK))]
  transfers between devices with their start and end apart: 7 -> 0, of which waited for: 5 -> 0; matrix products, arithmetic and copies ran while one was open for 18% -> 0% of each run, Pallas kernels for 0% -> 0%
where the time goes in v1:
time: 49.9 us; the launch traced here: 49.7 us
  Pallas kernels  47.6 us (95%)
  local copies, waits for them, and re-layouts  2.06 us (4%)
    pallas_call x1, Pallas kernels, body(): pl.pallas_call(functools.partial(kernel, row_count, col_count, relay), ou...  47.6 us
    unnamed x1, local copies, waits for them, and re-layouts  2.06 us

profile of v1, /device:TPU:0, one launch (start us, length us, event | category | flops | bytes accessed | tf_op | source)
XLA Modules:
  0.0 49.7 jit_solution(6074315370858818294)
XLA Ops:
  0.0 47.6 %shard_map.55 = bf16[3,256,512]{2,1,0:T(8,128)(2,1)} custom-call(s32[3]{0:T(128)} %branch.1, s32[8,8]{1,0:T(8,128)} %p0_occ.1, s32[8,8]{1,0:T(8,128)} %p1_occ.1, bf16[1536,512]{1,0:T(8,128)(2,1)} %strip_in.1, bf16[3,256,512]{2,1,0:T(8,128)(2,1)} %tile_in.1), custom_call_target="tpu_custom_call" | custom-call | flops 2214592512 | bytes 4194304 | tf_op jit(solution)/shard_map/pallas_call | solution.py:218
  47.6 2.1 %copy.7 = bf16[3,256,512]{2,1,0:T(8,128)(2,1)} copy(bf16[3,256,512]{2,1,0:T(8,128)(2,1)} %shard_map.55) | data formatting | bytes 1572864

commit v2 on v1

--- a/solution.py
+++ b/solution.py
@@ -59,9 +59,13 @@
             device_id=device, device_id_type=MESH,
         )
 
-    def z_copy(which, d):
-        return remote(mine.at[d], rows.at[3 * which, d], row_send.at[which, d],
-                      row_recv.at[which, d], row_id(2 - 4 * which))
+    def first_copy(d):
+        return remote(mine.at[d], rows.at[3 - 3 * odd, d], row_send.at[0, d],
+                      row_recv.at[0, d], row_id(4 * odd - 2))
+
+    def last_copy(d):
+        return remote(mine.at[d], rows.at[3 * odd, d], row_send.at[1, d],
+                      row_recv.at[1, d], row_id(2 - 4 * odd))
 
     def own_copy(d):
         return remote(mine.at[d], rows.at[1 + odd, d], row_send.at[2, d],
@@ -83,9 +87,7 @@
 
     if relay:
         for d in range(disp):
-            z_copy(0, d).start()
-            z_copy(1, d).start()
-        for d in range(disp):
+            first_copy(d).start()
             own_copy(d).start()
     else:
         for d in range(disp):
@@ -98,6 +100,23 @@
 
     def fact_copy(k):
         return remote(fact, fact, fact_send.at[k], fact_recv.at[0], col_id(k + 1))
+
+    core_odd = lax.rem(c, 2)
+    core = col_id(1 - 2 * core_odd)
+    across = lax.rem(owner + 2, col_count)
+
+    def fact_core():
+        return remote(fact, fact, fact_send.at[0], fact_recv.at[0], core)
+
+    def fact_across():
+        return remote(fact, fact, fact_send.at[1], fact_recv.at[0], col_id(2))
+
+    def col_core():
+        return remote(mine, cols.at[core_odd], col_send.at[0], col_recv.at[0], core)
+
+    def col_across():
+        return remote(mine, cols.at[1 - core_odd], col_send.at[1], col_recv.at[1],
+                      col_id(2 * core_odd - 1))
 
     @pl.when(c == owner)
     def _():
@@ -105,11 +124,18 @@
             for i in range(row_blocks):
                 block = strip[pl.ds(offset + k * BLK, BLK), pl.ds(offset + i * BLK, BLK)]
                 fact[i * BLK:(i + 1) * BLK, k * BLK:(k + 1) * BLK] = block.T
-        for k in range(col_count - 1):
-            fact_copy(k).start()
-
-    for k in range(len(col_far)):
-        col_copy(k).start()
+        if relay:
+            fact_across().start()
+            fact_core().start()
+        else:
+            for k in range(col_count - 1):
+                fact_copy(k).start()
+
+    if relay:
+        col_core().start()
+    else:
+        for k in range(len(col_far)):
+            col_copy(k).start()
 
     def col_add(tile, distance, first=False):
         at = pl.ds(pl.multiple_of((distance + col_span) * width, BLK), width)
@@ -147,31 +173,39 @@
         def _():
             fact_copy(0).wait_recv()
 
+        if relay:
+            @pl.when(c == across)
+            def _():
+                fact_core().start()
+
     col_add(mine, 0, first=True)
     if relay:
         def forward(d):
-            remote(mine.at[d], rows.at[0, d], row_send.at[0, d],
-                   row_recv.at[1 - odd, d], partner).wait_recv()
+            first_copy(d).wait_recv()
             relay_copy(d).start()
 
+        col_core().wait_recv()
+        col_add(cols.at[1 - core_odd], 1 - 2 * core_odd)
         forward(0)
+        col_across().start()
         wait_fact()
         row_add(mine, 0)
         forward(1)
-        for k in range(len(col_far)):
-            col_copy(len(col_far) - 1 - k).wait_recv()
-            col_add(cols.at[k], col_far[k])
+        first_copy(1).wait_send()
+        last_copy(0).start()
+        forward(2)
+        first_copy(2).wait_send()
+        for d in range(1, disp):
+            last_copy(d).start()
         for d in range(disp):
             own_copy(d).wait_recv()
         row_add(rows.at[2 - odd], 1 - 2 * odd)
-        for d in range(2, disp):
-            forward(d)
         row_add(rows.at[3 - 3 * odd], 2 - 4 * odd)
-        for d in range(disp):
-            remote(mine.at[d], rows.at[0, d], row_send.at[0, d],
-                   row_recv.at[odd, d], partner).wait_recv()
-        row_add(rows.at[3 * odd], 4 * odd - 2)
-        for d in range(disp):
+        col_across().wait_recv()
+        col_add(cols.at[core_odd], 2 * core_odd - 1)
+        for d in range(disp):
+            last_copy(d).wait_recv()
+            acc[d] += row_term(rows.at[3 * odd], 4 * odd - 2, d)
             relay_copy(d).wait_recv()
             acc[d] += row_term(rows.at[1 + odd], 2 * odd - 1, d)
             finish(d)
@@ -188,22 +222,33 @@
         for d in range(disp):
             finish(d)
 
-    for k in range(len(col_far)):
-        col_copy(k).wait_send()
-    for d in range(disp):
-        if relay:
-            z_copy(0, d).wait_send()
-            z_copy(1, d).wait_send()
+    if relay:
+        col_core().wait_send()
+        col_across().wait_send()
+        first_copy(0).wait_send()
+        for d in range(disp):
+            last_copy(d).wait_send()
             own_copy(d).wait_send()
             relay_copy(d).wait_send()
-        else:
+
+        @pl.when(c == owner)
+        def _():
+            fact_across().wait_send()
+
+        @pl.when(jnp.logical_or(c == owner, c == across))
+        def _():
+            fact_core().wait_send()
+    else:
+        for k in range(len(col_far)):
+            col_copy(k).wait_send()
+        for d in range(disp):
             for k in range(len(row_far)):
                 row_copy(k, d).wait_send()
 
-    @pl.when(c == owner)
-    def _():
-        for k in range(col_count - 1):
-            fact_copy(k).wait_send()
+        @pl.when(c == owner)
+        def _():
+            for k in range(col_count - 1):
+                fact_copy(k).wait_send()
 
 
 def body(sp2_branch, p0_occupancy, p1_occupancy, p0_columns, p1_tiles):
@@ -213,7 +258,7 @@
     half = (strip_rows - width) // 2
     row_slots, col_slots = 2 * (half // height), 2 * (half // width)
     bf16 = jnp.bfloat16
-    relay = row_slots == 4
+    relay = row_slots == 4 and col_slots == 2 and col_count == 4 and disp == 3
     flops = 2 * disp * height * width * (strip_rows + height + 2 * half)
     return pl.pallas_call(
         functools.partial(kernel, row_count, col_count, relay),

time: 49.9 us -> 46.7 us (0.936)
  Pallas kernels: 47.6 us -> 44.5 us
    pallas_call x1, Pallas kernels: 47.6 us -> 44.5 us  [body(): pl.pallas_call(functools.partial(kernel, row_count, col_count, relay), ou...]
where the time goes in v2:
time: 46.7 us; the launch traced here: 46.5 us
  Pallas kernels  44.5 us (95%)
  local copies, waits for them, and re-layouts  2.06 us (4%)
    pallas_call x1, Pallas kernels, body(): pl.pallas_call(functools.partial(kernel, row_count, col_count, relay), ou...  44.5 us
    unnamed x1, local copies, waits for them, and re-layouts  2.06 us

profile of v2, /device:TPU:0, one launch (start us, length us, event | category | flops | bytes accessed | tf_op | source)
XLA Modules:
  0.0 46.5 jit_solution(5413297641150143462)
XLA Ops:
  0.0 44.5 %shard_map.55 = bf16[3,256,512]{2,1,0:T(8,128)(2,1)} custom-call(s32[3]{0:T(128)} %branch.1, s32[8,8]{1,0:T(8,128)} %p0_occ.1, s32[8,8]{1,0:T(8,128)} %p1_occ.1, bf16[1536,512]{1,0:T(8,128)(2,1)} %strip_in.1, bf16[3,256,512]{2,1,0:T(8,128)(2,1)} %tile_in.1), custom_call_target="tpu_custom_call" | custom-call | flops 2214592512 | bytes 4194304 | tf_op jit(solution)/shard_map/pallas_call | solution.py:263
  44.5 2.1 %copy.7 = bf16[3,256,512]{2,1,0:T(8,128)(2,1)} copy(bf16[3,256,512]{2,1,0:T(8,128)(2,1)} %shard_map.55) | data formatting | bytes 1572864

commit v3 on v2

--- a/solution.py
+++ b/solution.py
@@ -11,20 +11,19 @@
 MESH = pl.DeviceIdType.MESH
 
 
-def mask_into(dst, src, occ, row_block, col_block, total):
-    rows, cols = src.shape[-2], src.shape[-1]
+def mask_blocks(values, occ, row_block, col_block, total):
+    rows, cols = values.shape
     for i in range(rows // BLK):
         for j in range(cols // BLK):
             weight = occ[lax.rem(row_block + i + total, total), col_block + j].astype(jnp.float32)
             at = (slice(i * BLK, (i + 1) * BLK), slice(j * BLK, (j + 1) * BLK))
-            at = (slice(None),) * (len(src.shape) - 2) + at
-            dst[at] = (src[at].astype(jnp.float32) * weight).astype(jnp.bfloat16)
+            values[at] = (values[at].astype(jnp.float32) * weight).astype(jnp.bfloat16)
 
 
 def kernel(
     row_count, col_count, relay,
     branch, p0_occ, p1_occ, strip_in, tile_in, out,
-    mine, strip, fact, acc, cols, rows,
+    load_sem, mine, strip, fact, acc, cols, rows,
     col_send, col_recv, row_send, row_recv, fact_send, fact_recv,
 ):
     disp, height, width = tile_in.shape
@@ -50,8 +49,14 @@
     for device in greeted:
         pl.semaphore_signal(barrier, inc=1, device_id=device, device_id_type=MESH)
 
-    mask_into(mine, tile_in, p1_occ, r * row_blocks, c * col_blocks, total)
-    pl.semaphore_wait(barrier, len(greeted))
+    loads = [pltpu.make_async_copy(tile_in.at[d], mine.at[d], load_sem.at[d]) for d in range(disp)]
+    loads.append(pltpu.make_async_copy(strip_in, strip, load_sem.at[disp]))
+    for load in loads:
+        load.start()
+
+    def load_tile(d):
+        loads[d].wait()
+        mask_blocks(mine.at[d], p1_occ, r * row_blocks, c * col_blocks, total)
 
     def remote(src, dst, send, recv, device):
         return pltpu.make_async_remote_copy(
@@ -87,14 +92,21 @@
 
     if relay:
         for d in range(disp):
+            load_tile(d)
+            if d == 0:
+                pl.semaphore_wait(barrier, len(greeted))
             first_copy(d).start()
             own_copy(d).start()
     else:
         for d in range(disp):
+            load_tile(d)
+        pl.semaphore_wait(barrier, len(greeted))
+        for d in range(disp):
             for k in range(len(row_far)):
                 row_copy(k, d).start()
 
-    mask_into(strip, strip_in, p0_occ, c * col_blocks - half, c * col_blocks, total)
+    loads[disp].wait()
+    mask_blocks(strip, p0_occ, c * col_blocks - half, c * col_blocks, total)
     owner = r * row_blocks // col_blocks
     offset = pl.multiple_of((r * row_blocks - owner * col_blocks) * BLK, BLK)
 
@@ -262,11 +274,12 @@
     flops = 2 * disp * height * width * (strip_rows + height + 2 * half)
     return pl.pallas_call(
         functools.partial(kernel, row_count, col_count, relay),
-        out_shape=jax.ShapeDtypeStruct(p1_tiles.shape, bf16),
+        out_shape=pltpu.VMEM(p1_tiles.shape, bf16),
         in_specs=[pl.BlockSpec(memory_space=pltpu.SMEM)] * 3
-        + [pl.BlockSpec(memory_space=pltpu.VMEM)] * 2,
+        + [pl.BlockSpec(memory_space=pl.ANY)] * 2,
         out_specs=pl.BlockSpec(memory_space=pltpu.VMEM),
         scratch_shapes=[
+            pltpu.SemaphoreType.DMA((disp + 1,)),
             pltpu.VMEM((disp, height, width), bf16),
             pltpu.VMEM(p0_columns.shape, bf16),
             pltpu.VMEM((height, height + 2 * half), bf16),

time: 46.7 us -> 43.9 us (0.940)
  Pallas kernels: 44.5 us -> 42.8 us
  local copies, waits for them, and re-layouts: 2.06 us -> 0.88 us
    pallas_call x1, Pallas kernels: 44.5 us -> 42.8 us  [body(): pl.pallas_call(functools.partial(kernel, row_count, col_count, relay), ou...]
    unnamed x1, local copies, waits for them, and re-layouts: 2.06 us -> 0.88 us
where the time goes in v3:
time: 43.9 us; the launch traced here: 43.7 us
  Pallas kernels  42.8 us (97%)
  local copies, waits for them, and re-layouts  0.88 us (2%)
    pallas_call x1, Pallas kernels, body(): pl.pallas_call(functools.partial(kernel, row_count, col_count, relay), ou...  42.8 us
    unnamed x1, local copies, waits for them, and re-layouts  0.88 us

profile of v3, /device:TPU:0, one launch (start us, length us, event | category | flops | bytes accessed | tf_op | source)
XLA Modules:
  0.0 43.7 jit_solution(14929787470643336009)
XLA Ops:
  0.0 42.8 %shard_map.55 = bf16[3,256,512]{2,1,0:T(8,128)(2,1)S(1)} custom-call(s32[3]{0:T(128)} %branch.1, s32[8,8]{1,0:T(8,128)} %p0_occ.1, s32[8,8]{1,0:T(8,128)} %p1_occ.1, bf16[1536,512]{1,0:T(8,128)(2,1)} %strip_in.1, bf16[3,256,512]{2,1,0:T(8,128)(2,1)} %tile_in.1), custom_call_target="tpu_custom_call" | custom-call | flops 2214592512 | bytes 4194304 | tf_op jit(solution)/shard_map/pallas_call | solution.py:275
  42.8 0.9 %copy.7 = bf16[3,256,512]{2,1,0:T(8,128)(2,1)} copy(bf16[3,256,512]{2,1,0:T(8,128)(2,1)S(1)} %shard_map.55) | data formatting | bytes 1572864

commit v4 on v3

--- a/solution.py
+++ b/solution.py
@@ -198,17 +198,14 @@
 
         col_core().wait_recv()
         col_add(cols.at[1 - core_odd], 1 - 2 * core_odd)
-        forward(0)
-        col_across().start()
-        wait_fact()
-        row_add(mine, 0)
-        forward(1)
-        first_copy(1).wait_send()
-        last_copy(0).start()
-        forward(2)
-        first_copy(2).wait_send()
-        for d in range(1, disp):
+        for d in range(disp):
+            forward(d)
             last_copy(d).start()
+            if d == 0:
+                col_across().start()
+            if d == 1:
+                wait_fact()
+                row_add(mine, 0)
         for d in range(disp):
             own_copy(d).wait_recv()
         row_add(rows.at[2 - odd], 1 - 2 * odd)
@@ -237,8 +234,8 @@
     if relay:
         col_core().wait_send()
         col_across().wait_send()
-        first_copy(0).wait_send()
-        for d in range(disp):
+        for d in range(disp):
+            first_copy(d).wait_send()
             last_copy(d).wait_send()
             own_copy(d).wait_send()
             relay_copy(d).wait_send()

time: 43.9 us -> 43.9 us (level)
  no operation moved by 1% of the time
where the time goes in v4:
time: 43.9 us; the launch traced here: 43.7 us
  Pallas kernels  42.8 us (97%)
  local copies, waits for them, and re-layouts  0.88 us (2%)
    pallas_call x1, Pallas kernels, body(): pl.pallas_call(functools.partial(kernel, row_count, col_count, relay), ou...  42.8 us
    unnamed x1, local copies, waits for them, and re-layouts  0.88 us

profile of v4, /device:TPU:0, one launch (start us, length us, event | category | flops | bytes accessed | tf_op | source)
XLA Modules:
  0.0 43.7 jit_solution(8411507750378287499)
XLA Ops:
  0.0 42.8 %shard_map.55 = bf16[3,256,512]{2,1,0:T(8,128)(2,1)S(1)} custom-call(s32[3]{0:T(128)} %branch.1, s32[8,8]{1,0:T(8,128)} %p0_occ.1, s32[8,8]{1,0:T(8,128)} %p1_occ.1, bf16[1536,512]{1,0:T(8,128)(2,1)} %strip_in.1, bf16[3,256,512]{2,1,0:T(8,128)(2,1)} %tile_in.1), custom_call_target="tpu_custom_call" | custom-call | flops 2214592512 | bytes 4194304 | tf_op jit(solution)/shard_map/pallas_call | solution.py:272
  42.8 0.9 %copy.7 = bf16[3,256,512]{2,1,0:T(8,128)(2,1)} copy(bf16[3,256,512]{2,1,0:T(8,128)(2,1)S(1)} %shard_map.55) | data formatting | bytes 1572864

commit v5 on v4

--- a/solution.py
+++ b/solution.py
@@ -145,6 +145,7 @@
 
     if relay:
         col_core().start()
+        col_across().start()
     else:
         for k in range(len(col_far)):
             col_copy(k).start()
@@ -201,8 +202,6 @@
         for d in range(disp):
             forward(d)
             last_copy(d).start()
-            if d == 0:
-                col_across().start()
             if d == 1:
                 wait_fact()
                 row_add(mine, 0)

time: 43.9 us -> 43.9 us (level)
  no operation moved by 1% of the time
where the time goes in v5:
time: 43.9 us; the launch traced here: 43.7 us
  Pallas kernels  42.8 us (97%)
  local copies, waits for them, and re-layouts  0.88 us (2%)
    pallas_call x1, Pallas kernels, body(): pl.pallas_call(functools.partial(kernel, row_count, col_count, relay), ou...  42.8 us
    unnamed x1, local copies, waits for them, and re-layouts  0.88 us

profile of v5, /device:TPU:0, one launch (start us, length us, event | category | flops | bytes accessed | tf_op | source)
XLA Modules:
  0.0 43.7 jit_solution(9215147717711158859)
XLA Ops:
  0.0 42.8 %shard_map.55 = bf16[3,256,512]{2,1,0:T(8,128)(2,1)S(1)} custom-call(s32[3]{0:T(128)} %branch.1, s32[8,8]{1,0:T(8,128)} %p0_occ.1, s32[8,8]{1,0:T(8,128)} %p1_occ.1, bf16[1536,512]{1,0:T(8,128)(2,1)} %strip_in.1, bf16[3,256,512]{2,1,0:T(8,128)(2,1)} %tile_in.1), custom_call_target="tpu_custom_call" | custom-call | flops 2214592512 | bytes 4194304 | tf_op jit(solution)/shard_map/pallas_call | solution.py:271
  42.8 0.9 %copy.7 = bf16[3,256,512]{2,1,0:T(8,128)(2,1)} copy(bf16[3,256,512]{2,1,0:T(8,128)(2,1)S(1)} %shard_map.55) | data formatting | bytes 1572864
